TPU v7x, 512 devices: a whole 4x8x8 slice. The times are simulated.
512 devices in a mesh: users: 64 (over y, z_hi, x), cand: 8 (over z_lo, core).
Axes of the slice: x: 4, y: 8, z: 8 (z_hi: 2, z_lo: 4; z = z_hi * 4 + z_lo), core: 2. Of those that a mesh axis runs over, the one named last changes fastest.
Arguments:
- candidate_rows: bfloat16 [32768, 1024], P(('users', 'cand')), may hold values from -6 to 6
- weight_in: bfloat16 [2, 1024, 8, 512], P(None, None, 'cand'), may hold values from -0.1875 to 0.1875
- weight_out: bfloat16 [2, 8, 128, 1024], P(None, 'cand'), may hold values from -0.1875 to 0.1875
- history_cache: bfloat16 [2, 2, 8192, 8, 128], P(None, None, 'users', 'cand'), may hold values from -6 to 6
- block_user: int32 [64], replicated, may hold values from 0 to 15, as said below
- block_offset: int32 [64], replicated, may hold values from 0 to 31, as said below
- history_length: int32 [16], replicated, may hold values from 1 to 4096, as said below
- candidate_count: int32 [16], replicated, may hold values from 1 to 16384, as said below
Outputs:
- scored_rows: bfloat16 [32768, 1024], P(('users', 'cand'))
Inputs may be any that keep to these rules, and one draw needn't show every extreme that they name: `block_user`: every one of the 16 users owns at least one block; the blocks of one user may stand anywhere; exactly one user owns 64 / 2 blocks, every other user fewer. `block_offset`: the blocks of a user that owns b blocks carry the offsets 0 to b - 1, each once. `history_length`: a user that owns b blocks has more than (b - 1) * 128 and at most b * 128 history rows. `candidate_count`: the counts sum to 32768; the rows of one user are consecutive, users in increasing order.
All inputs are finite; a program needn't handle non-finite values.
Results may differ from a plain program's by a relative error of at most 0.027.
Values may be sent and summed in bfloat16 or wider, within the bound.
A program may use at most 64 MiB of HBM per device.

v0:
```python
import math
import jax
import jax.numpy as jnp
from jax import lax
from jax.sharding import PartitionSpec as P

BLOCK = 128


def body(
    candidate_rows,
    weight_in,
    weight_out,
    history_cache,
    block_user,
    block_offset,
    history_length,
    candidate_count,
):
    own_rows, model_width = candidate_rows.shape
    layers, model_again, heads_here, packed = weight_in.shape
    head_dim = packed // 4
    cand_devices = lax.axis_size("cand")
    row_count = own_rows * cand_devices
    score_scale = 1.0 / math.sqrt(head_dim)
    user_count = history_length.shape[0]
    users_all = jnp.arange(user_count, dtype=jnp.int32)
    user_ends = jnp.cumsum(candidate_count)
    group_rows = lax.axis_index("users") * row_count + jnp.arange(row_count, dtype=jnp.int32)
    cand_user = jnp.sum((group_rows[:, None] >= user_ends[None, :]).astype(jnp.int32), axis=1)
    step_rows = 4 * BLOCK

    def block_term(accumulated, key_value, piece_start, queries):
        span_rows = key_value.shape[1]
        span_blocks = span_rows // BLOCK
        first_block = piece_start // BLOCK
        owners = lax.dynamic_slice_in_dim(block_user, first_block, span_blocks)
        places = lax.dynamic_slice_in_dim(block_offset, first_block, span_blocks)
        row_user = jnp.broadcast_to(owners[:, None], (span_blocks, BLOCK)).reshape(span_rows)
        row_place = (places[:, None] * BLOCK + jnp.arange(BLOCK, dtype=jnp.int32)[None, :]).reshape(
            span_rows
        )
        row_length = jnp.sum(
            jnp.where(row_user[:, None] == users_all[None, :], history_length[None, :], 0), axis=1
        )
        visible = (cand_user[:, None] == row_user[None, :]) & (row_place < row_length)[None, :]
        scores = (
            jnp.einsum("rhd,nhd->hrn", queries, key_value[0], preferred_element_type=jnp.float32)
            * score_scale
        )
        weights = jnp.where(visible[None], jax.nn.silu(scores), 0.0).astype(jnp.bfloat16)
        return accumulated + jnp.einsum(
            "hrn,nhd->rhd", weights, key_value[1], preferred_element_type=jnp.float32
        )

    current_own = candidate_rows
    for layer_index in range(layers):
        project_segment = lax.all_gather(current_own, "cand", axis=0, tiled=True)
        flat = weight_in[layer_index].reshape(model_width, heads_here * packed)
        mixed = jnp.dot(project_segment, flat, preferred_element_type=jnp.float32)
        projected = (
            jax.nn.silu(mixed)
            .astype(jnp.bfloat16)
            .reshape(project_segment.shape[0], heads_here, 4, head_dim)
        )
        gate_part = projected[:, :, 0]
        values_part = projected[:, :, 1]
        queries = projected[:, :, 2]
        keys_part = projected[:, :, 3]
        own_score = (
            jnp.sum(queries.astype(jnp.float32) * keys_part.astype(jnp.float32), axis=-1)
            * score_scale
        )
        own_weight = jax.nn.silu(own_score).astype(jnp.bfloat16)
        own_term = own_weight.astype(jnp.float32)[..., None] * values_part.astype(jnp.float32)
        empty_sum = jnp.zeros((row_count, heads_here, head_dim), jnp.float32)
        segment = lax.all_gather(history_cache[layer_index], "users", axis=1, tiled=True)
        fold_span_rows = segment.shape[1]
        turns = fold_span_rows // step_rows

        def advance(position, running):
            sliced = lax.dynamic_slice_in_dim(segment, position * step_rows, step_rows, 1)
            return block_term(running, sliced, position * step_rows, queries)

        attended = lax.fori_loop(0, turns, advance, empty_sum)
        attended = attended + own_term
        centred = attended - jnp.mean(attended, axis=-1, keepdims=True)
        variance = jnp.mean(centred * centred, axis=-1, keepdims=True)
        gated = (centred * lax.rsqrt(variance + 1e-05) * gate_part.astype(jnp.float32)).astype(
            jnp.bfloat16
        )
        partial_out = jnp.dot(
            gated.reshape(row_count, heads_here * head_dim),
            weight_out[layer_index].reshape(heads_here * head_dim, model_width),
            preferred_element_type=jnp.float32,
        )
        shared = lax.psum_scatter(
            partial_out.astype(jnp.bfloat16), "cand", scatter_dimension=0, tiled=True
        ).astype(jnp.float32)
        current_own = (current_own.astype(jnp.float32) + shared).astype(jnp.bfloat16)
    return current_own


def solution(mesh):
    placed = (
        P(("users", "cand"), None),
        P(None, None, "cand", None),
        P(None, "cand", None, None),
        P(None, None, "users", "cand", None),
        P(),
        P(),
        P(),
        P(),
    )
    return jax.shard_map(
        body, mesh=mesh, in_specs=placed, out_specs=P(("users", "cand"), None), check_vma=False
    )
```

profile of v0, /device:TPU:2, one launch (start us, length us, event | category | flops | bytes accessed | tf_op | source)
XLA Modules:
  0.0 570.2 jit_solution(17218734392977073218)
XLA Ops:
  9.9 44.5 %all-gather.7.cloned.1.call-done = bf16[512,1024]{1,0:T(8,128)(2,1)} async-done(((bf16[64,1024]{1,0:T(8,128)(2,1)}), bf16[512,1024]{1,0:T(8,128)(2,1)}) %all-gather.7.cloned.1.call-update) | async-done | bytes 1048592 | tf_op jit(solution)/shard_map/all_gather | solution.py:58
  54.4 2.4 multiply_convert_fusion.1
  57.1 159.0 %all-gather.11.cloned.1.call-done = bf16[1,2,8192,1,128]{4,2,1,3,0:T(8,128)(2,1)} async-done(((bf16[1,2,128,1,128]{4,2,1,3,0:T(8,128)(2,1)}), bf16[1,2,8192,1,128]{4,2,1,3,0:T(8,128)(2,1)}) %all-gather.11.cloned.1.call-update) | async-done | bytes 4194320 | tf_op jit(solution)/shard_map/all_gather | solution.py:77
  216.1 35.4 %while.32 = (s32[]{:T(128)}, f32[512,1,128]{0,2,1:T(8,128)S(1)}, bf16[2,8192,1,128]{3,1,2,0:T(8,128)(2,1)}, s32[512]{0:T(512)S(1)}, s32[64]{0:T(128)S(1)}, /*ind...) while((s32[]{:T(128)}, f32[512,1,128]{0,2,1:T(8,128)S(1)}, ...), condition=%wide.region_4.5_spmd.clone, body=%wide.region_2.4_spmd.clone.sunk | while | flops 136733216 | bytes 933431 | solution.py:85
  218.7 1.8 fusion.82
  225.4 1.8 fusion.82
  227.6 1.8 fusion.82
  234.2 1.8 fusion.82
  236.4 1.8 fusion.82
  253.2 34.7 %reduce-scatter.3.cloned.1.call-done = bf16[64,1024]{1,0:T(8,128)(2,1)} async-done(((bf16[512,1024]{1,0:T(8,128)(2,1)}), bf16[64,1024]{1,0:T(8,128)(2,1)}) %reduce-scatter.3.cloned.1.call-update) | async-done | bytes 131088 | tf_op jit(solution)/shard_map/reduce_scatter | solution.py:97
  290.1 38.4 %all-gather.9.cloned.1.call-done = bf16[512,1024]{1,0:T(8,128)(2,1)} async-done(((bf16[64,1024]{1,0:T(8,128)(2,1)}), bf16[512,1024]{1,0:T(8,128)(2,1)}) %all-gather.9.cloned.1.call-update) | async-done | bytes 1048592 | tf_op jit(solution)/shard_map/all_gather | solution.py:58
  328.5 2.4 multiply_convert_fusion
  331.1 158.8 %all-gather.13.cloned.1.call-done = bf16[1,2,8192,1,128]{4,2,1,3,0:T(8,128)(2,1)} async-done(((bf16[1,2,128,1,128]{4,2,1,3,0:T(8,128)(2,1)}), bf16[1,2,8192,1,128]{4,2,1,3,0:T(8,128)(2,1)}) %all-gather.13.cloned.1.call-update) | async-done | bytes 4194320 | tf_op jit(solution)/shard_map/all_gather | solution.py:77
  490.0 35.3 %while.33 = (s32[]{:T(128)}, f32[512,1,128]{0,2,1:T(8,128)S(1)}, bf16[2,8192,1,128]{3,1,2,0:T(8,128)(2,1)}, s32[512]{0:T(512)S(1)}, s32[64]{0:T(128)S(1)}, /*ind...) while((s32[]{:T(128)}, f32[512,1,128]{0,2,1:T(8,128)S(1)}, ...), condition=%wide.region_11.12_spmd.clone, body=%wide.region_9.11_spmd.clone.sunk | while | flops 136733216 | bytes 933431 | solution.py:85
  490.4 1.8 fusion.84
  492.6 1.8 fusion.84
  497.0 1.8 fusion.84
  501.4 1.8 fusion.84
  505.8 1.8 fusion.84
  510.3 1.8 fusion.84
  514.7 1.8 fusion.84
  519.1 1.8 fusion.84
  523.5 1.8 fusion.84
  527.0 34.8 %reduce-scatter.5.cloned.1.call-done = bf16[64,1024]{1,0:T(8,128)(2,1)} async-done(((bf16[512,1024]{1,0:T(8,128)(2,1)}), bf16[64,1024]{1,0:T(8,128)(2,1)}) %reduce-scatter.5.cloned.1.call-update) | async-done | bytes 131088 | tf_op jit(solution)/shard_map/reduce_scatter | solution.py:97
  (230 shorter events, 55.1 us)
Async XLA Ops:
  6.5 47.9 %all-gather.7.cloned.1.call-start = ((), (), s32[]{:S(2)}) async-start(), calls=%async_computation.2 | async-start | bytes 1179648 | tf_op jit(solution)/shard_map/all_gather | solution.py:58
  7.3 208.8 %all-gather.11.cloned.1.call-start = ((), (), s32[]{:S(2)}) async-start(), calls=%async_computation.6 | async-start | bytes 4259840 | tf_op jit(solution)/shard_map/all_gather | solution.py:77
  8.9 279.0 %reduce-scatter.3.cloned.1.call-start = ((), (), s32[]{:S(2)}) async-start(), calls=%async_computation.3 | async-start | bytes 1179648 | tf_op jit(solution)/shard_map/reduce_scatter | solution.py:97
  9.9 206.2 %copy-start.3 = (s32[16]{0:T(128)S(1)}, s32[16]{0:T(128)}, u32[]{:S(2)}) copy-start(s32[16]{0:T(128)} %param.18) | copy-start | bytes 196
  9.9 206.2 %copy-start.4 = (s32[64]{0:T(128)S(1)}, s32[64]{0:T(128)}, u32[]{:S(2)}) copy-start(s32[64]{0:T(128)} %param.16) | copy-start | bytes 772
  9.9 206.2 %copy-start.5 = (s32[64]{0:T(128)S(1)}, s32[64]{0:T(128)}, u32[]{:S(2)}) copy-start(s32[64]{0:T(128)} %param.17) | copy-start | bytes 772
  216.1 35.5 %copy-start.2 = (bf16[2,1,128,1024]{3,2,1,0:T(8,128)(2,1)S(1)}, bf16[2,1,128,1024]{3,2,1,0:T(8,128)(2,1)}, u32[]{:S(2)}) copy-start(bf16[2,1,128,1024]{3,2,1,0:T(8,128)(2,1)} %param.14) | copy-start | bytes 1572868
  216.1 71.8 %copy-start.1 = (bf16[64,1024]{1,0:T(8,128)(2,1)S(1)}, bf16[64,1024]{1,0:T(8,128)(2,1)}, u32[]{:S(2)}) copy-start(bf16[64,1024]{1,0:T(8,128)(2,1)} %param.12) | copy-start | bytes 393220
  253.1 75.4 %all-gather.9.cloned.1.call-start = ((), (), s32[]{:S(2)}) async-start(), calls=%async_computation.4 | async-start | bytes 1179648 | tf_op jit(solution)/shard_map/all_gather | solution.py:58
  289.5 200.5 %all-gather.13.cloned.1.call-start = ((), (), s32[]{:S(2)}) async-start(), calls=%async_computation.7 | async-start | bytes 4259840 | tf_op jit(solution)/shard_map/all_gather | solution.py:77
  290.1 271.7 %reduce-scatter.5.cloned.1.call-start = ((), (), s32[]{:S(2)}) async-start(), calls=%async_computation.5 | async-start | bytes 1179648 | tf_op jit(solution)/shard_map/reduce_scatter | solution.py:97
  490.0 71.8 %copy-start = (bf16[64,1024]{1,0:T(8,128)(2,1)S(1)}, bf16[64,1024]{1,0:T(8,128)(2,1)}, u32[]{:S(2)}) copy-start(bf16[64,1024]{1,0:T(8,128)(2,1)} %add_convert_fusion.1) | copy-start | bytes 393220
Sparse Core Ops, SparseCore 0:
  9.4 44.9 all-gather.6
  58.8 157.2 all-gather.10
  253.2 34.5 reduce-scatter.2
  289.8 38.6 all-gather.8
  332.7 157.2 all-gather.12
  527.1 34.6 reduce-scatter.4
where the time goes:
time: 571 us; the launch traced here: 570 us
  waiting for transfers between devices  471 us (82%)
  matrix products  64.3 us (11%)
  between operations  13.6 us (2%)
  other arithmetic  11.6 us (2%)
  local copies, waits for them, and re-layouts  7.34 us (1%)
    all_gather x2, waiting for transfers between devices, body(): lax.all_gather(history_cache[layer_index], 'users', axis=1, tiled=True)  318 us
    all_gather x2, waiting for transfers between devices, body(): project_segment = lax.all_gather(current_own, 'cand', axis=0, tiled=True)  82.9 us
    reduce_scatter x2, waiting for transfers between devices, body(): lax.psum_scatter(partial_out.astype(jnp.bfloat16), 'cand', scatter_dimens...  69.5 us
    dot_general x32, matrix products, block_term(): jnp.einsum('hrn,nhd->rhd', weights, key_value[1], preferred_element_type=...  56.5 us
  transfers between devices with their start and end apart: 6, of which 6 were waited for; matrix products, arithmetic and copies ran while one was open for 1% of the time, Pallas kernels for 0%

commit v1 on v0

--- a/solution.py
+++ b/solution.py
@@ -1,3 +1,4 @@
+import functools
 import math
 import jax
 import jax.numpy as jnp
@@ -5,6 +6,15 @@
 from jax.sharding import PartitionSpec as P
 
 BLOCK = 128
+
+
+def prepare_the_tails(panel, group_axis):
+    return jnp.concatenate(
+        lax.all_to_all(jnp.stack([panel] * lax.axis_size(group_axis)), group_axis, 0, 0), 1
+    )
+
+
+_resolve_kinds = functools.partial(prepare_the_tails, group_axis="users")
 
 
 def body(
@@ -74,7 +84,7 @@
         own_weight = jax.nn.silu(own_score).astype(jnp.bfloat16)
         own_term = own_weight.astype(jnp.float32)[..., None] * values_part.astype(jnp.float32)
         empty_sum = jnp.zeros((row_count, heads_here, head_dim), jnp.float32)
-        segment = lax.all_gather(history_cache[layer_index], "users", axis=1, tiled=True)
+        segment = _resolve_kinds(history_cache[layer_index])
         fold_span_rows = segment.shape[1]
         turns = fold_span_rows // step_rows
 

time: 571 us -> 408 us (0.71)
  waiting for transfers between devices: 471 us -> 258 us
  starting transfers between devices: 0.2 us -> 36.1 us
  local copies, waits for them, and re-layouts: 7.34 us -> 21.5 us
    all_gather x2 -> x0, waiting for transfers between devices: 318 us -> none  [body(): lax.all_gather(history_cache[layer_index], 'users', axis=1, tiled=True)]
    all_gather x2, waiting for transfers between devices: 82.9 us -> 146 us  [body(): project_segment = lax.all_gather(current_own, 'cand', axis=0, tiled=True)]
    reduce_scatter x2, waiting for transfers between devices: 69.5 us -> 111 us  [body(): lax.psum_scatter(partial_out.astype(jnp.bfloat16), 'cand', scatter_dimens...]
    all_to_all x0 -> x2, starting transfers between devices: none -> 35.9 us  [prepare_the_tails(): lax.all_to_all(jnp.stack([panel] * lax.axis_size(group_axis)), group_axis...]
    all_to_all x0 -> x2, local copies, waits for them, and re-layouts: none -> 9.48 us  [prepare_the_tails(): lax.all_to_all(jnp.stack([panel] * lax.axis_size(group_axis)), group_axis...]
  transfers between devices with their start and end apart: 6 -> 6, of which waited for: 6 -> 4; matrix products, arithmetic and copies ran while one was open for 1% -> 12% of each run, Pallas kernels for 0% -> 0%
where the time goes in v1:
time: 408 us; the launch traced here: 407 us
  waiting for transfers between devices  258 us (63%)
  matrix products  64.3 us (16%)
  starting transfers between devices  36.1 us (9%)
  local copies, waits for them, and re-layouts  21.5 us (5%)
  between operations  13.3 us (3%)
  other arithmetic  11.6 us (3%)
    all_gather x2, waiting for transfers between devices, body(): project_segment = lax.all_gather(current_own, 'cand', axis=0, tiled=True)  146 us
    reduce_scatter x2, waiting for transfers between devices, body(): lax.psum_scatter(partial_out.astype(jnp.bfloat16), 'cand', scatter_dimens...  111 us
    dot_general x32, matrix products, block_term(): jnp.einsum('hrn,nhd->rhd', weights, key_value[1], preferred_element_type=...  56.4 us
    all_to_all x2, starting transfers between devices, prepare_the_tails(): lax.all_to_all(jnp.stack([panel] * lax.axis_size(group_axis)), group_axis...  35.9 us
    all_to_all x2, local copies, waits for them, and re-layouts, prepare_the_tails(): lax.all_to_all(jnp.stack([panel] * lax.axis_size(group_axis)), group_axis...  9.48 us
  transfers between devices with their start and end apart: 6, of which 4 were waited for; matrix products, arithmetic and copies ran while one was open for 12% of the time, Pallas kernels for 0%

profile of v1, /device:TPU:2, one launch (start us, length us, event | category | flops | bytes accessed | tf_op | source)
XLA Modules:
  0.0 406.6 jit_solution(12979235742452881655)
XLA Ops:
  7.4 3.0 stack.6
  10.4 19.4 %all-to-all-start = ((bf16[64,2,128,1,128]{4,2,1,3,0:T(8,128)(2,1)}), bf16[64,2,128,1,128]{4,2,1,3,0:T(8,128)(2,1)}, u32[]{:S(2)}, u32[]{:S(2)}) async-start(bf16[64,2,128,1,128]{4,2,1,3,0:T(8,128)(2,1)} %stack.6), calls=%async_computation | async-start | bytes 8388608 | tf_op jit(solution)/shard_map/all_to_all | solution.py:13
  30.9 109.4 %all-gather.3.cloned.1.call-done = bf16[512,1024]{1,0:T(8,128)(2,1)} async-done(((bf16[64,1024]{1,0:T(8,128)(2,1)}), bf16[512,1024]{1,0:T(8,128)(2,1)}) %all-gather.3.cloned.1.call-update) | async-done | bytes 1048592 | tf_op jit(solution)/shard_map/all_gather | solution.py:68
  140.3 2.4 multiply_convert_fusion.1
  143.0 3.0 stack.7
  146.0 16.5 %all-to-all-start.1 = ((bf16[64,2,128,1,128]{4,2,1,3,0:T(8,128)(2,1)}), bf16[64,2,128,1,128]{4,2,1,3,0:T(8,128)(2,1)}, u32[]{:S(2)}, u32[]{:S(2)}) async-start(bf16[64,2,128,1,128]{4,2,1,3,0:T(8,128)(2,1)} %stack.7), calls=%async_computation.2 | async-start | bytes 8388608 | tf_op jit(solution)/shard_map/all_to_all | solution.py:13
  162.6 4.7 %copy.24 = bf16[64,2,128,1,128]{4,2,0,1,3:T(8,128)(2,1)} copy(bf16[64,2,128,1,128]{4,2,1,3,0:T(8,128)(2,1)} %all-to-all-done) | data formatting | bytes 8388608 | tf_op jit(solution)/shard_map/all_to_all | solution.py:13
  167.4 35.3 %while.32 = (s32[]{:T(128)}, f32[512,1,128]{0,2,1:T(8,128)S(1)}, bf16[2,8192,1,128]{3,1,2,0:T(8,128)(2,1)}, s32[512]{0:T(512)S(1)}, s32[64]{0:T(128)S(1)}, /*ind...) while((s32[]{:T(128)}, f32[512,1,128]{0,2,1:T(8,128)S(1)}, ...), condition=%wide.region_4.5_spmd.clone, body=%wide.region_2.4_spmd.clone.sunk | while | flops 136733216 | bytes 933431 | solution.py:95
  176.7 1.8 fusion.81
  185.5 1.8 fusion.81
  194.3 1.8 fusion.81
  204.5 71.1 %reduce-scatter.3.cloned.1.call-done = bf16[64,1024]{1,0:T(8,128)(2,1)} async-done(((bf16[512,1024]{1,0:T(8,128)(2,1)}), bf16[64,1024]{1,0:T(8,128)(2,1)}) %reduce-scatter.3.cloned.1.call-update) | async-done | bytes 131088 | tf_op jit(solution)/shard_map/reduce_scatter | solution.py:107
  277.3 4.7 %copy.28 = bf16[64,2,128,1,128]{4,2,0,1,3:T(8,128)(2,1)} copy(bf16[64,2,128,1,128]{4,2,1,3,0:T(8,128)(2,1)} %all-to-all-done.1) | data formatting | bytes 8388608 | tf_op jit(solution)/shard_map/all_to_all | solution.py:13
  282.1 37.0 %all-gather.5.cloned.1.call-done = bf16[512,1024]{1,0:T(8,128)(2,1)} async-done(((bf16[64,1024]{1,0:T(8,128)(2,1)}), bf16[512,1024]{1,0:T(8,128)(2,1)}) %all-gather.5.cloned.1.call-update) | async-done | bytes 1048592 | tf_op jit(solution)/shard_map/all_gather | solution.py:68
  319.1 2.4 multiply_convert_fusion
  321.7 35.4 %while.33 = (s32[]{:T(128)}, f32[512,1,128]{0,2,1:T(8,128)S(1)}, bf16[2,8192,1,128]{3,1,2,0:T(8,128)(2,1)}, s32[512]{0:T(512)S(1)}, s32[64]{0:T(128)S(1)}, /*ind...) while((s32[]{:T(128)}, f32[512,1,128]{0,2,1:T(8,128)S(1)}, ...), condition=%wide.region_11.12_spmd.clone, body=%wide.region_9.11_spmd.clone.sunk | while | flops 136733216 | bytes 933431 | solution.py:95
  328.8 1.8 fusion.83
  333.2 1.8 fusion.83
  337.6 1.8 fusion.83
  342.1 1.8 fusion.83
  346.5 1.8 fusion.83
  350.9 1.8 fusion.83
  355.3 1.8 fusion.83
  358.8 39.7 %reduce-scatter.5.cloned.1.call-done = bf16[64,1024]{1,0:T(8,128)(2,1)} async-done(((bf16[512,1024]{1,0:T(8,128)(2,1)}), bf16[64,1024]{1,0:T(8,128)(2,1)}) %reduce-scatter.5.cloned.1.call-update) | async-done | bytes 131088 | tf_op jit(solution)/shard_map/reduce_scatter | solution.py:107
  (234 shorter events, 60.3 us)
Async XLA Ops:
  10.4 20.2 %copy-start.4 = (s32[16]{0:T(128)S(1)}, s32[16]{0:T(128)}, u32[]{:S(2)}) copy-start(s32[16]{0:T(128)} %param.19) | copy-start | bytes 196
  10.4 132.6 %all-to-all-start = ((bf16[64,2,128,1,128]{4,2,1,3,0:T(8,128)(2,1)}), bf16[64,2,128,1,128]{4,2,1,3,0:T(8,128)(2,1)}, u32[]{:S(2)}, u32[]{:S(2)}) async-start(bf16[64,2,128,1,128]{4,2,1,3,0:T(8,128)(2,1)} %stack.6), calls=%async_computation | async-start | bytes 8388608 | tf_op jit(solution)/shard_map/all_to_all | solution.py:13
  29.8 110.5 %all-gather.3.cloned.1.call-start = ((), (), s32[]{:S(2)}) async-start(), calls=%async_computation.4 | async-start | bytes 1179648 | tf_op jit(solution)/shard_map/all_gather | solution.py:68
  146.0 131.3 %all-to-all-start.1 = ((bf16[64,2,128,1,128]{4,2,1,3,0:T(8,128)(2,1)}), bf16[64,2,128,1,128]{4,2,1,3,0:T(8,128)(2,1)}, u32[]{:S(2)}, u32[]{:S(2)}) async-start(bf16[64,2,128,1,128]{4,2,1,3,0:T(8,128)(2,1)} %stack.7), calls=%async_computation.2 | async-start | bytes 8388608 | tf_op jit(solution)/shard_map/all_to_all | solution.py:13
  162.5 4.8 %copy-start.3 = (s32[16]{0:T(128)S(1)}, s32[16]{0:T(128)}, u32[]{:S(2)}) copy-start(s32[16]{0:T(128)} %param.18) | copy-start | bytes 196
  162.5 4.8 %copy-start.5 = (s32[64]{0:T(128)S(1)}, s32[64]{0:T(128)}, u32[]{:S(2)}) copy-start(s32[64]{0:T(128)} %param.16) | copy-start | bytes 772
  162.6 4.8 %copy-start.6 = (s32[64]{0:T(128)S(1)}, s32[64]{0:T(128)}, u32[]{:S(2)}) copy-start(s32[64]{0:T(128)} %param.17) | copy-start | bytes 772
  162.6 113.1 %reduce-scatter.3.cloned.1.call-start = ((), (), s32[]{:S(2)}) async-start(), calls=%async_computation.5 | async-start | bytes 1179648 | tf_op jit(solution)/shard_map/reduce_scatter | solution.py:107
  167.4 35.5 %copy-start.2 = (bf16[2,1,128,1024]{3,2,1,0:T(8,128)(2,1)S(1)}, bf16[2,1,128,1024]{3,2,1,0:T(8,128)(2,1)}, u32[]{:S(2)}) copy-start(bf16[2,1,128,1024]{3,2,1,0:T(8,128)(2,1)} %param.14) | copy-start | bytes 1572868
  167.4 108.3 %copy-start.1 = (bf16[64,1024]{1,0:T(8,128)(2,1)S(1)}, bf16[64,1024]{1,0:T(8,128)(2,1)}, u32[]{:S(2)}) copy-start(bf16[64,1024]{1,0:T(8,128)(2,1)} %param.12) | copy-start | bytes 393220
  204.5 114.6 %all-gather.5.cloned.1.call-start = ((), (), s32[]{:S(2)}) async-start(), calls=%async_computation.6 | async-start | bytes 1179648 | tf_op jit(solution)/shard_map/all_gather | solution.py:68
  277.3 121.2 %reduce-scatter.5.cloned.1.call-start = ((), (), s32[]{:S(2)}) async-start(), calls=%async_computation.7 | async-start | bytes 1179648 | tf_op jit(solution)/shard_map/reduce_scatter | solution.py:107
  321.7 76.7 %copy-start = (bf16[64,1024]{1,0:T(8,128)(2,1)S(1)}, bf16[64,1024]{1,0:T(8,128)(2,1)}, u32[]{:S(2)}) copy-start(bf16[64,1024]{1,0:T(8,128)(2,1)} %add_convert_fusion.1) | copy-start | bytes 393220
Sparse Core Ops, SparseCore 0:
  32.7 107.5 all-gather.2
  204.6 71.0 reduce-scatter.2
  277.7 41.2 all-gather.4
  358.9 39.4 reduce-scatter.4
